TPU v7x, 256 devices: a whole 4x4x8 slice. The times are simulated.
256 devices in a mesh: samp: 32 (over z, y), rows: 8 (over x, core).
Axes of the slice: x: 4, y: 4, z: 8, core: 2. Of those that a mesh axis runs over, the one named last changes fastest.
Arguments:
- samples: float32 [32, 640, 4480], P('samp', 'rows'), may hold values from -6 to 6
- truth_field: float32 [640, 4480], P('rows', 'samp'), may hold values from -6 to 6
Outputs:
- contrast_fine: float32 [32, 640, 4480], P('samp', 'rows')
- contrast_half: float32 [32, 320, 2240], P('samp', 'rows')
- contrast_quarter: float32 [32, 160, 1120], P('samp', 'rows')
- contrast_eighth: float32 [32, 80, 560], P('samp', 'rows')
- similarity_coarse: float32 [32, 40, 280], P('samp', 'rows')
All inputs are finite; a program needn't handle non-finite values.
Results may differ from a plain program's by a relative error of at most 0.00002.
Values sent between devices are 32-bit elements; how exact they have to be, the bound alone decides.
No kernel may reach another device: no remote copies, remote signals or barrier semaphores. Data moves between devices by JAX's collectives and lax.ppermute only.
A program may use at most 128 MiB of HBM per device.

v0:
```python
import jax
import jax.numpy as jnp
from jax import lax
from jax.sharding import PartitionSpec as P

small_one = 0.0001
small_two = 0.0009


def with_halo(block, sides, width):
    for axis, dim in sides:
        count = lax.axis_size(axis)
        forward = [(i, i + 1) for i in range(count - 1)]
        backward = [(target, source) for source, target in forward]
        low = lax.ppermute(
            lax.slice_in_dim(block, block.shape[dim] - width, None, axis=dim), axis, forward
        )
        high = lax.ppermute(lax.slice_in_dim(block, 0, width, axis=dim), axis, backward)
        block = jnp.concatenate([low, block, high], axis=dim)
    return block


def window():
    offsets = jnp.arange(11).astype(jnp.float32) - 5.0
    shaped = jnp.exp(-offsets * offsets / 4.5)
    return shaped / jnp.sum(shaped)


def smooth(padded, weights):
    row_count = padded.shape[-2] - 10
    column_count = padded.shape[-1]
    vertical = weights[0] * padded[..., 0:row_count, :]
    for tap_index in range(1, 11):
        vertical = vertical + weights[tap_index] * padded[..., tap_index : tap_index + row_count, :]
    widths = [(0, 0)] * (padded.ndim - 1) + [(5, 5)]
    widened = jnp.pad(vertical, widths)
    result = weights[0] * widened[..., 0:column_count]
    for tap_index in range(1, 11):
        result = result + weights[tap_index] * widened[..., tap_index : tap_index + column_count]
    return result


def halve_grid(field):
    upper = field[..., 0::2, :]
    lower = field[..., 1::2, :]
    return 0.25 * (upper[..., 0::2] + upper[..., 1::2] + lower[..., 0::2] + lower[..., 1::2])


def level_maps(sample_pad, truth_pad, weights, coarsest):
    truth_wide = truth_pad[None]
    stacked = jnp.stack(
        [
            sample_pad,
            truth_wide,
            sample_pad * sample_pad,
            truth_wide * truth_wide,
            sample_pad * truth_wide,
        ],
        axis=0,
    )
    moments = lax.map(lambda field: smooth(field, weights), stacked)
    mean_x = moments[0]
    mean_y = moments[1]
    var_x = moments[2] - mean_x * mean_x
    var_y = moments[3] - mean_y * mean_y
    covar = moments[4] - mean_x * mean_y
    contrast = (2.0 * covar + small_two) / (var_x + var_y + small_two)
    if coarsest:
        luminance = (2.0 * mean_x * mean_y + small_one) / (
            mean_x * mean_x + mean_y * mean_y + small_one
        )
        return luminance * contrast
    return contrast


def local(samples, truth_field):
    weights = window()
    truth_levels = []
    sample_levels = []
    truth_rows = lax.all_gather(truth_field, "samp", axis=1, tiled=True)
    current = jnp.concatenate([truth_rows[None], samples], axis=0)
    for level_index in range(5):
        if level_index > 0:
            current = halve_grid(current)
        padded = with_halo(current, (("rows", 1),), 5)
        truth_levels.append(padded[0])
        sample_levels.append(padded[1:])
    return tuple(
        (
            level_maps(
                sample_levels[level_index], truth_levels[level_index], weights, level_index == 4
            )
            for level_index in range(5)
        )
    )


def solution(mesh):
    placed = (P("samp", "rows", None), P("rows", "samp"))
    return jax.shard_map(
        local,
        mesh=mesh,
        in_specs=placed,
        out_specs=(
            P("samp", "rows", None),
            P("samp", "rows", None),
            P("samp", "rows", None),
            P("samp", "rows", None),
            P("samp", "rows", None),
        ),
        check_vma=False,
    )
```

profile of v0, /device:TPU:1, one launch (start us, length us, event | category | flops | bytes accessed | tf_op | source)
XLA Modules:
  0.0 804.6 jit_solution(12436675204161090629)
XLA Ops:
  9.2 80.0 %all-gather.3.cloned.1.call-done = f32[32,140,80]{2,1,0:T(8,128)} async-done(((f32[1,140,80]{2,1,0:T(8,128)}), f32[32,140,80]{2,1,0:T(8,128)}) %all-gather.3.cloned.1.call-update) | async-done | bytes 1433616 | tf_op jit(solution)/shard_map/all_gather | solution.py:80
  96.0 7.6 slice.1230
  103.6 30.2 %slice.1231 = f32[2,40,2240]{2,1,0:T(8,128)} slice(f32[2,40,4480]{2,1,0:T(8,128)} %slice.1230), slice={[0:2:1], [0:40:1], [0:4480:2]} | slice | bytes 1433600 | tf_op jit(solution)/shard_map/slice | solution.py:46
  133.8 30.2 %slice.1232 = f32[2,40,2240]{2,1,0:T(8,128)} slice(f32[2,40,4480]{2,1,0:T(8,128)} %slice.1230), slice={[0:2:1], [0:40:1], [1:4480:2]} | slice | bytes 1433600 | tf_op jit(solution)/shard_map/slice | solution.py:46
  164.0 7.6 slice.1233
  171.6 30.4 %slice.1234 = f32[2,40,2240]{2,1,0:T(8,128)} slice(f32[2,40,4480]{2,1,0:T(8,128)} %slice.1233), slice={[0:2:1], [0:40:1], [0:4480:2]} | slice | bytes 1433600 | tf_op jit(solution)/shard_map/slice | solution.py:46
  201.9 30.2 %slice.1235 = f32[2,40,2240]{2,1,0:T(8,128)} slice(f32[2,40,4480]{2,1,0:T(8,128)} %slice.1233), slice={[0:2:1], [0:40:1], [1:4480:2]} | slice | bytes 1433600 | tf_op jit(solution)/shard_map/slice | solution.py:46
  304.2 80.6 %while.64 = (s32[]{:T(128)}, f32[5,1,5,280]{3,0,2,1:T(8,128)}, f32[11]{0:T(128)S(1)}, f32[5,1,15,280]{3,2,1,0:T(8,128)S(1)}, s32[]{:T(128)}, /*index=5*/s32[]{:T(128)}) while((s32[]{:T(128)}, f32[5,1,5,280]{3,0,2,1:T(8,128)}, f32[11]{0:T(128)S(1)}, f32[5,1,15,280]{3,2,1,0:T(8,128)S(1)}, s32[]{:T(128)}, /*index=5*/s32[]{:T(128)}) %tuple.190), condition=%wide.region_10.11_spmd, body=%wide.region_9.10_spmd.sunk | while | flops 58802 | bytes 134653 | solution.py:61
  392.2 83.3 %while.63 = (s32[]{:T(128)}, f32[5,1,10,560]{3,0,2,1:T(8,128)}, f32[11]{0:T(128)S(1)}, f32[5,1,20,560]{3,2,1,0:T(8,128)S(1)}, s32[]{:T(128)}, /*index=5*/s32[]{:T(128)}) while((s32[]{:T(128)}, f32[5,1,10,560]{3,0,2,1:T(8,128)}, f32[11]{0:T(128)S(1)}, f32[5,1,20,560]{3,2,1,0:T(8,128)S(1)}, s32[]{:T(128)}, /*index=5*/s32[]{:T(128)}) %tuple.195), condition=%wide.region_8.9_spmd, body=%wide.region_7.8_spmd.sunk | while | flops 235202 | bytes 493053 | solution.py:61
  481.6 94.7 %while.62 = (s32[]{:T(128)}, f32[5,1,20,1120]{3,0,2,1:T(8,128)}, f32[11]{0:T(128)S(1)}, f32[5,1,30,1120]{3,2,1,0:T(8,128)}, s32[]{:T(128)}, /*index=5*/s32[]{:T(128)}) while((s32[]{:T(128)}, f32[5,1,20,1120]{3,0,2,1:T(8,128)}, f32[11]{0:T(128)S(1)}, f32[5,1,30,1120]{3,2,1,0:T(8,128)}, s32[]{:T(128)}, /*index=5*/s32[]{:T(128)}) %tuple.201), condition=%wide.region_6.7_spmd, body=%wide.region_5.6_spmd.sunk | while | flops 940802 | bytes 1881853 | solution.py:61
  582.8 90.1 %while.61 = (s32[]{:T(128)}, f32[5,1,40,2240]{3,2,1,0:T(8,128)}, f32[11]{0:T(128)S(1)}, f32[5,1,50,2240]{3,2,1,0:T(8,128)}, s32[]{:T(128)}) while((s32[]{:T(128)}, f32[5,1,40,2240]{3,2,1,0:T(8,128)}, f32[11]{0:T(128)S(1)}, f32[5,1,50,2240]{3,2,1,0:T(8,128)}, s32[]{:T(128)}) %tuple.200), condition=%wide.region_4.5_spmd, body=%wide.region_3.4_spmd.sunk | while | flops 3763202 | bytes 5930181 | solution.py:61
  584.6 7.5 fusion.123
  592.0 8.8 %bitcast_dynamic-update-slice_fusion.25 = f32[5,1,40,2240]{3,2,1,0:T(8,128)} fusion(f32[5,1,40,2240]{3,2,1,0:T(8,128)} %get-tuple-element.634, s32[]{:T(128)} %get-tuple-element.633, f32[1,40,2240]{2,1,0:T(8,128)S(1)} %fusion.123, f32[]{:T(128)} %bitcast.279, f32[]{:T(128)} %bitcast.280, f32[]{:T(128)} %bitcast.281, f32[]{:T(128)} %bitcast.282, ...), kind=kLoop, calls=%fused_computation.56.clone.1 | loop fusion | flops 1881600 | bytes 733184 | tf_op jit(solution)/shard_map/while/body/jit(dynamic_update_index_in_dim)/dynamic_update_slice | solution.py:61
  602.6 7.5 fusion.123
  610.0 8.8 %bitcast_dynamic-update-slice_fusion.25 = f32[5,1,40,2240]{3,2,1,0:T(8,128)} fusion(f32[5,1,40,2240]{3,2,1,0:T(8,128)} %get-tuple-element.634, s32[]{:T(128)} %get-tuple-element.633, f32[1,40,2240]{2,1,0:T(8,128)S(1)} %fusion.123, f32[]{:T(128)} %bitcast.279, f32[]{:T(128)} %bitcast.280, f32[]{:T(128)} %bitcast.281, f32[]{:T(128)} %bitcast.282, ...), kind=kLoop, calls=%fused_computation.56.clone.1 | loop fusion | flops 1881600 | bytes 733184 | tf_op jit(solution)/shard_map/while/body/jit(dynamic_update_index_in_dim)/dynamic_update_slice | solution.py:61
  620.6 7.5 fusion.123
  628.0 8.8 %bitcast_dynamic-update-slice_fusion.25 = f32[5,1,40,2240]{3,2,1,0:T(8,128)} fusion(f32[5,1,40,2240]{3,2,1,0:T(8,128)} %get-tuple-element.634, s32[]{:T(128)} %get-tuple-element.633, f32[1,40,2240]{2,1,0:T(8,128)S(1)} %fusion.123, f32[]{:T(128)} %bitcast.279, f32[]{:T(128)} %bitcast.280, f32[]{:T(128)} %bitcast.281, f32[]{:T(128)} %bitcast.282, ...), kind=kLoop, calls=%fused_computation.56.clone.1 | loop fusion | flops 1881600 | bytes 733184 | tf_op jit(solution)/shard_map/while/body/jit(dynamic_update_index_in_dim)/dynamic_update_slice | solution.py:61
  638.6 7.5 fusion.123
  646.1 8.8 %bitcast_dynamic-update-slice_fusion.25 = f32[5,1,40,2240]{3,2,1,0:T(8,128)} fusion(f32[5,1,40,2240]{3,2,1,0:T(8,128)} %get-tuple-element.634, s32[]{:T(128)} %get-tuple-element.633, f32[1,40,2240]{2,1,0:T(8,128)S(1)} %fusion.123, f32[]{:T(128)} %bitcast.279, f32[]{:T(128)} %bitcast.280, f32[]{:T(128)} %bitcast.281, f32[]{:T(128)} %bitcast.282, ...), kind=kLoop, calls=%fused_computation.56.clone.1 | loop fusion | flops 1881600 | bytes 733184 | tf_op jit(solution)/shard_map/while/body/jit(dynamic_update_index_in_dim)/dynamic_update_slice | solution.py:61
  656.6 7.5 fusion.123
  664.1 8.8 %bitcast_dynamic-update-slice_fusion.25 = f32[5,1,40,2240]{3,2,1,0:T(8,128)} fusion(f32[5,1,40,2240]{3,2,1,0:T(8,128)} %get-tuple-element.634, s32[]{:T(128)} %get-tuple-element.633, f32[1,40,2240]{2,1,0:T(8,128)S(1)} %fusion.123, f32[]{:T(128)} %bitcast.279, f32[]{:T(128)} %bitcast.280, f32[]{:T(128)} %bitcast.281, f32[]{:T(128)} %bitcast.282, ...), kind=kLoop, calls=%fused_computation.56.clone.1 | loop fusion | flops 1881600 | bytes 733184 | tf_op jit(solution)/shard_map/while/body/jit(dynamic_update_index_in_dim)/dynamic_update_slice | solution.py:61
  680.5 112.1 %while.60 = (s32[]{:T(128)}, f32[5,1,80,4480]{3,2,1,0:T(8,128)}, f32[11]{0:T(128)S(1)}, f32[5,1,90,4480]{3,2,1,0:T(8,128)}, s32[]{:T(128)}) while((s32[]{:T(128)}, f32[5,1,80,4480]{3,2,1,0:T(8,128)}, f32[11]{0:T(128)S(1)}, f32[5,1,90,4480]{3,2,1,0:T(8,128)}, s32[]{:T(128)}) %tuple.199), condition=%wide.region_2.3_spmd, body=%wide.region_1.2_spmd.sunk | while | flops 15052802 | bytes 23302340 | solution.py:61
  682.7 8.7 %fusion.121 = f32[1,80,4480]{2,1,0:T(8,128)S(1)} fusion(f32[1,90,4480]{2,1,0:T(8,128)S(1)} %dynamic-slice_bitcast_fusion.10, f32[]{:T(128)} %bitcast.266, f32[]{:T(128)} %bitcast.267, f32[]{:T(128)} %bitcast.268, f32[]{:T(128)} %bitcast.269, f32[]{:T(128)} %bitcast.270, f32[]{:T(128)} %bitcast.271, f32[]{:T(128)} %bitcast.272, f32[]{:T(128)} %bitcast.273, ...), kind=kLoop, calls=%fused_computation.2.clone.1 | loop fusion | flops 7526400 | bytes 17203244 | tf_op jit(solution)/shard_map/while/body/eval_jaxpr/add | solution.py:34
  691.4 11.5 %bitcast_dynamic-update-slice_fusion.24 = f32[5,1,80,4480]{3,2,1,0:T(8,128)} fusion(f32[5,1,80,4480]{3,2,1,0:T(8,128)} %get-tuple-element.619, s32[]{:T(128)} %get-tuple-element.618, f32[1,80,4480]{2,1,0:T(8,128)S(1)} %fusion.121, f32[]{:T(128)} %bitcast.266, f32[]{:T(128)} %bitcast.267, f32[]{:T(128)} %bitcast.268, f32[]{:T(128)} %bitcast.269, ...), kind=kLoop, calls=%fused_computation.22.clone.1 | loop fusion | flops 7526400 | bytes 2873344 | tf_op jit(solution)/shard_map/while/body/jit(dynamic_update_index_in_dim)/dynamic_update_slice | solution.py:61
  705.2 8.7 %fusion.121 = f32[1,80,4480]{2,1,0:T(8,128)S(1)} fusion(f32[1,90,4480]{2,1,0:T(8,128)S(1)} %dynamic-slice_bitcast_fusion.10, f32[]{:T(128)} %bitcast.266, f32[]{:T(128)} %bitcast.267, f32[]{:T(128)} %bitcast.268, f32[]{:T(128)} %bitcast.269, f32[]{:T(128)} %bitcast.270, f32[]{:T(128)} %bitcast.271, f32[]{:T(128)} %bitcast.272, f32[]{:T(128)} %bitcast.273, ...), kind=kLoop, calls=%fused_computation.2.clone.1 | loop fusion | flops 7526400 | bytes 17203244 | tf_op jit(solution)/shard_map/while/body/eval_jaxpr/add | solution.py:34
  713.9 11.5 %bitcast_dynamic-update-slice_fusion.24 = f32[5,1,80,4480]{3,2,1,0:T(8,128)} fusion(f32[5,1,80,4480]{3,2,1,0:T(8,128)} %get-tuple-element.619, s32[]{:T(128)} %get-tuple-element.618, f32[1,80,4480]{2,1,0:T(8,128)S(1)} %fusion.121, f32[]{:T(128)} %bitcast.266, f32[]{:T(128)} %bitcast.267, f32[]{:T(128)} %bitcast.268, f32[]{:T(128)} %bitcast.269, ...), kind=kLoop, calls=%fused_computation.22.clone.1 | loop fusion | flops 7526400 | bytes 2873344 | tf_op jit(solution)/shard_map/while/body/jit(dynamic_update_index_in_dim)/dynamic_update_slice | solution.py:61
  727.6 8.7 %fusion.121 = f32[1,80,4480]{2,1,0:T(8,128)S(1)} fusion(f32[1,90,4480]{2,1,0:T(8,128)S(1)} %dynamic-slice_bitcast_fusion.10, f32[]{:T(128)} %bitcast.266, f32[]{:T(128)} %bitcast.267, f32[]{:T(128)} %bitcast.268, f32[]{:T(128)} %bitcast.269, f32[]{:T(128)} %bitcast.270, f32[]{:T(128)} %bitcast.271, f32[]{:T(128)} %bitcast.272, f32[]{:T(128)} %bitcast.273, ...), kind=kLoop, calls=%fused_computation.2.clone.1 | loop fusion | flops 7526400 | bytes 17203244 | tf_op jit(solution)/shard_map/while/body/eval_jaxpr/add | solution.py:34
  736.3 11.5 %bitcast_dynamic-update-slice_fusion.24 = f32[5,1,80,4480]{3,2,1,0:T(8,128)} fusion(f32[5,1,80,4480]{3,2,1,0:T(8,128)} %get-tuple-element.619, s32[]{:T(128)} %get-tuple-element.618, f32[1,80,4480]{2,1,0:T(8,128)S(1)} %fusion.121, f32[]{:T(128)} %bitcast.266, f32[]{:T(128)} %bitcast.267, f32[]{:T(128)} %bitcast.268, f32[]{:T(128)} %bitcast.269, ...), kind=kLoop, calls=%fused_computation.22.clone.1 | loop fusion | flops 7526400 | bytes 2873344 | tf_op jit(solution)/shard_map/while/body/jit(dynamic_update_index_in_dim)/dynamic_update_slice | solution.py:61
  750.0 8.7 %fusion.121 = f32[1,80,4480]{2,1,0:T(8,128)S(1)} fusion(f32[1,90,4480]{2,1,0:T(8,128)S(1)} %dynamic-slice_bitcast_fusion.10, f32[]{:T(128)} %bitcast.266, f32[]{:T(128)} %bitcast.267, f32[]{:T(128)} %bitcast.268, f32[]{:T(128)} %bitcast.269, f32[]{:T(128)} %bitcast.270, f32[]{:T(128)} %bitcast.271, f32[]{:T(128)} %bitcast.272, f32[]{:T(128)} %bitcast.273, ...), kind=kLoop, calls=%fused_computation.2.clone.1 | loop fusion | flops 7526400 | bytes 17203244 | tf_op jit(solution)/shard_map/while/body/eval_jaxpr/add | solution.py:34
  758.7 11.5 %bitcast_dynamic-update-slice_fusion.24 = f32[5,1,80,4480]{3,2,1,0:T(8,128)} fusion(f32[5,1,80,4480]{3,2,1,0:T(8,128)} %get-tuple-element.619, s32[]{:T(128)} %get-tuple-element.618, f32[1,80,4480]{2,1,0:T(8,128)S(1)} %fusion.121, f32[]{:T(128)} %bitcast.266, f32[]{:T(128)} %bitcast.267, f32[]{:T(128)} %bitcast.268, f32[]{:T(128)} %bitcast.269, ...), kind=kLoop, calls=%fused_computation.22.clone.1 | loop fusion | flops 7526400 | bytes 2873344 | tf_op jit(solution)/shard_map/while/body/jit(dynamic_update_index_in_dim)/dynamic_update_slice | solution.py:61
  772.5 8.7 %fusion.121 = f32[1,80,4480]{2,1,0:T(8,128)S(1)} fusion(f32[1,90,4480]{2,1,0:T(8,128)S(1)} %dynamic-slice_bitcast_fusion.10, f32[]{:T(128)} %bitcast.266, f32[]{:T(128)} %bitcast.267, f32[]{:T(128)} %bitcast.268, f32[]{:T(128)} %bitcast.269, f32[]{:T(128)} %bitcast.270, f32[]{:T(128)} %bitcast.271, f32[]{:T(128)} %bitcast.272, f32[]{:T(128)} %bitcast.273, ...), kind=kLoop, calls=%fused_computation.2.clone.1 | loop fusion | flops 7526400 | bytes 17203244 | tf_op jit(solution)/shard_map/while/body/eval_jaxpr/add | solution.py:34
  781.2 11.5 %bitcast_dynamic-update-slice_fusion.24 = f32[5,1,80,4480]{3,2,1,0:T(8,128)} fusion(f32[5,1,80,4480]{3,2,1,0:T(8,128)} %get-tuple-element.619, s32[]{:T(128)} %get-tuple-element.618, f32[1,80,4480]{2,1,0:T(8,128)S(1)} %fusion.121, f32[]{:T(128)} %bitcast.266, f32[]{:T(128)} %bitcast.267, f32[]{:T(128)} %bitcast.268, f32[]{:T(128)} %bitcast.269, ...), kind=kLoop, calls=%fused_computation.22.clone.1 | loop fusion | flops 7526400 | bytes 2873344 | tf_op jit(solution)/shard_map/while/body/jit(dynamic_update_index_in_dim)/dynamic_update_slice | solution.py:61
  (211 shorter events, 390.8 us)
Async XLA Ops:
  7.2 82.1 %all-gather.3.cloned.1.call-start = ((), (), s32[]{:S(2)}) async-start(), calls=%async_computation | async-start | bytes 2433024 | tf_op jit(solution)/shard_map/all_gather | solution.py:80
  92.0 2.3 copy-start
  277.0 21.6 %collective-permute-start.8 = (f32[2,5,280]{2,1,0:T(8,128)S(1)}, f32[2,5,280]{2,1,0:T(8,128)S(1)}, u32[]{:S(2)}, u32[]{:S(2)}) collective-permute-start(f32[2,5,280]{2,1,0:T(8,128)S(1)} %add_multiply_fusion.3), channel_id=1, source_target_pairs={{0,1},{1,2},{2,3},{3,4},{4,5},{5,6},{6,7},{8,9},{9,10},{10,11},{11... | collective-permute-start | bytes 33608 | tf_op jit(solution)/shard_map/ppermute | solution.py:15
  284.2 16.3 %collective-permute-start.9 = (f32[2,5,280]{2,1,0:T(8,128)S(1)}, f32[2,5,280]{2,1,0:T(8,128)S(1)}, u32[]{:S(2)}, u32[]{:S(2)}) collective-permute-start(f32[2,5,280]{2,1,0:T(8,128)S(1)} %add_multiply_fusion.3), channel_id=1, source_target_pairs={{1,0},{2,1},{3,2},{4,3},{5,4},{6,5},{7,6},{9,8},{10,9},{11,10},{12... | collective-permute-start | bytes 33608 | tf_op jit(solution)/shard_map/ppermute | solution.py:18
  289.3 97.2 %collective-permute-start.6 = (f32[2,5,560]{2,1,0:T(8,128)S(1)}, f32[2,5,560]{2,1,0:T(8,128)S(1)}, u32[]{:S(2)}, u32[]{:S(2)}) collective-permute-start(f32[2,5,560]{2,1,0:T(8,128)S(1)} %get-tuple-element.376), channel_id=1, source_target_pairs={{0,1},{1,2},{2,3},{3,4},{4,5},{5,6},{6,7},{8,9},{9,10},{10,11},{11... | collective-permute-start | bytes 67208 | tf_op jit(solution)/shard_map/ppermute | solution.py:15
  293.0 95.5 %collective-permute-start.7 = (f32[2,5,560]{2,1,0:T(8,128)S(1)}, f32[2,5,560]{2,1,0:T(8,128)S(1)}, u32[]{:S(2)}, u32[]{:S(2)}) collective-permute-start(f32[2,5,560]{2,1,0:T(8,128)S(1)} %get-tuple-element.377), channel_id=1, source_target_pairs={{1,0},{2,1},{3,2},{4,3},{5,4},{6,5},{7,6},{9,8},{10,9},{11,10},{12... | collective-permute-start | bytes 67208 | tf_op jit(solution)/shard_map/ppermute | solution.py:18
  294.9 182.8 %collective-permute-start.4 = (f32[2,5,1120]{2,1,0:T(8,128)}, f32[2,5,1120]{2,1,0:T(8,128)}, u32[]{:S(2)}, u32[]{:S(2)}) collective-permute-start(f32[2,5,1120]{2,1,0:T(8,128)} %get-tuple-element.374), channel_id=1, source_target_pairs={{0,1},{1,2},{2,3},{3,4},{4,5},{5,6},{6,7},{8,9},{9,10},{10,11},{11... | collective-permute-start | bytes 134408 | tf_op jit(solution)/shard_map/ppermute | solution.py:15
  298.6 181.0 %collective-permute-start.5 = (f32[2,5,1120]{2,1,0:T(8,128)S(1)}, f32[2,5,1120]{2,1,0:T(8,128)}, u32[]{:S(2)}, u32[]{:S(2)}) collective-permute-start(f32[2,5,1120]{2,1,0:T(8,128)S(1)} %get-tuple-element.375), channel_id=1, source_target_pairs={{1,0},{2,1},{3,2},{4,3},{5,4},{6,5},{7,6},{9,8},{10,9},{11,10},{12... | collective-permute-start | bytes 134408 | tf_op jit(solution)/shard_map/ppermute | solution.py:18
  300.5 279.2 %collective-permute-start.2 = (f32[2,5,2240]{2,1,0:T(8,128)}, f32[2,5,2240]{2,1,0:T(8,128)}, u32[]{:S(2)}, u32[]{:S(2)}) collective-permute-start(f32[2,5,2240]{2,1,0:T(8,128)} %get-tuple-element.372), channel_id=1, source_target_pairs={{0,1},{1,2},{2,3},{3,4},{4,5},{5,6},{6,7},{8,9},{9,10},{10,11},{11... | collective-permute-start | bytes 268808 | tf_op jit(solution)/shard_map/ppermute | solution.py:15
  386.5 193.2 %collective-permute-start.3 = (f32[2,5,2240]{2,1,0:T(8,128)}, f32[2,5,2240]{2,1,0:T(8,128)}, u32[]{:S(2)}, u32[]{:S(2)}) collective-permute-start(f32[2,5,2240]{2,1,0:T(8,128)} %get-tuple-element.373), channel_id=1, source_target_pairs={{1,0},{2,1},{3,2},{4,3},{5,4},{6,5},{7,6},{9,8},{10,9},{11,10},{12... | collective-permute-start | bytes 268808 | tf_op jit(solution)/shard_map/ppermute | solution.py:18
  388.4 286.8 %collective-permute-start = (f32[2,5,4480]{2,1,0:T(8,128)}, f32[2,5,4480]{2,1,0:T(8,128)}, u32[]{:S(2)}, u32[]{:S(2)}) collective-permute-start(f32[2,5,4480]{2,1,0:T(8,128)} %get-tuple-element.370), channel_id=1, source_target_pairs={{0,1},{1,2},{2,3},{3,4},{4,5},{5,6},{6,7},{8,9},{9,10},{10,11},{11... | collective-permute-start | bytes 537608 | tf_op jit(solution)/shard_map/ppermute | solution.py:15
  477.7 197.5 %collective-permute-start.1 = (f32[2,5,4480]{2,1,0:T(8,128)}, f32[2,5,4480]{2,1,0:T(8,128)S(1)}, u32[]{:S(2)}, u32[]{:S(2)}) collective-permute-start(f32[2,5,4480]{2,1,0:T(8,128)} %get-tuple-element.371), channel_id=1, source_target_pairs={{1,0},{2,1},{3,2},{4,3},{5,4},{6,5},{7,6},{9,8},{10,9},{11,10},{12... | collective-permute-start | bytes 537608 | tf_op jit(solution)/shard_map/ppermute | solution.py:18
  480.7 0.9 copy-start.3
  581.2 1.6 copy-start.2
  677.1 3.3 copy-start.1
Sparse Core Ops, SparseCore 0:
  10.6 78.6 all-gather.2
where the time goes:
time: 818 us; the launch traced here: 805 us
  other arithmetic  421 us (51%)
  local copies, waits for them, and re-layouts  256 us (31%)
  waiting for transfers between devices  80.7 us (10%)
  starting transfers between devices  31.4 us (4%)
  between operations  15 us (2%)
    add x25, other arithmetic, smooth(): vertical + weights[tap_index] * padded[..., tap_index:tap_index + row_cou...  185 us
    broadcast_in_dim x20, other arithmetic, level_maps(): moments = lax.map(lambda field: smooth(field, weights), stacked)  107 us
    dynamic_update_slice x10, other arithmetic, level_maps(): moments = lax.map(lambda field: smooth(field, weights), stacked)  101 us
    all_gather x1, waiting for transfers between devices, local(): truth_rows = lax.all_gather(truth_field, 'samp', axis=1, tiled=True)  80 us
    slice x4, local copies, waits for them, and re-layouts, halve_grid(): lower[..., 1::2]  39.5 us
    slice x4, local copies, waits for them, and re-layouts, halve_grid(): upper[..., 1::2]  39.1 us
    slice x4, local copies, waits for them, and re-layouts, halve_grid(): lower[..., 0::2]  39.1 us
    slice x4, local copies, waits for them, and re-layouts, halve_grid(): upper[..., 0::2] + upper[..., 1::2] + lower[..., 0::2] + lower[..., 1::2]  38.2 us
  transfers between devices with their start and end apart: 11, of which 1 were waited for; matrix products, arithmetic and copies ran while one was open for 45% of the time, Pallas kernels for 0%

commit v1 on v0

--- a/solution.py
+++ b/solution.py
@@ -77,7 +77,10 @@
     weights = window()
     truth_levels = []
     sample_levels = []
-    truth_rows = lax.all_gather(truth_field, "samp", axis=1, tiled=True)
+    truth_rows = jnp.concatenate(
+        lax.all_to_all(jnp.stack([truth_field for _ in range(lax.psum(1, "samp"))]), "samp", 0, 0),
+        axis=1,
+    )
     current = jnp.concatenate([truth_rows[None], samples], axis=0)
     for level_index in range(5):
         if level_index > 0:

time: 818 us -> 792 us (0.968)
  waiting for transfers between devices: 80.7 us -> 52.6 us
  between operations: 15 us -> 1.59 us
  starting transfers between devices: 31.4 us -> 41.9 us
    all_gather x1 -> x0, waiting for transfers between devices: 80 us -> none  [local(): truth_rows = lax.all_gather(truth_field, 'samp', axis=1, tiled=True)]
    all_to_all x0 -> x1, waiting for transfers between devices: none -> 52.6 us  [local(): lax.all_to_all(jnp.stack([truth_field for _ in range(lax.psum(1, 'samp'))...]
    all_to_all x0 -> x1, starting transfers between devices: none -> 12 us  [local(): lax.all_to_all(jnp.stack([truth_field for _ in range(lax.psum(1, 'samp'))...]
  transfers between devices with their start and end apart: 11 -> 11, of which waited for: 1 -> 1; matrix products, arithmetic and copies ran while one was open for 45% -> 47% of each run, Pallas kernels for 0% -> 0%
where the time goes in v1:
time: 792 us; the launch traced here: 778 us
  other arithmetic  424 us (54%)
  local copies, waits for them, and re-layouts  257 us (32%)
  waiting for transfers between devices  52.6 us (7%)
  starting transfers between devices  41.9 us (5%)
    add x25, other arithmetic, smooth(): vertical + weights[tap_index] * padded[..., tap_index:tap_index + row_cou...  187 us
    broadcast_in_dim x20, other arithmetic, level_maps(): moments = lax.map(lambda field: smooth(field, weights), stacked)  108 us
    dynamic_update_slice x10, other arithmetic, level_maps(): moments = lax.map(lambda field: smooth(field, weights), stacked)  102 us
    all_to_all x1, waiting for transfers between devices, local(): lax.all_to_all(jnp.stack([truth_field for _ in range(lax.psum(1, 'samp'))...  52.6 us
    slice x4, local copies, waits for them, and re-layouts, halve_grid(): lower[..., 1::2]  39.5 us
    slice x4, local copies, waits for them, and re-layouts, halve_grid(): upper[..., 1::2]  39.1 us
    slice x4, local copies, waits for them, and re-layouts, halve_grid(): lower[..., 0::2]  39.1 us
    slice x4, local copies, waits for them, and re-layouts, halve_grid(): upper[..., 0::2] + upper[..., 1::2] + lower[..., 0::2] + lower[..., 1::2]  38.2 us
  transfers between devices with their start and end apart: 11, of which 1 were waited for; matrix products, arithmetic and copies ran while one was open for 47% of the time, Pallas kernels for 0%

profile of v1, /device:TPU:1, one launch (start us, length us, event | category | flops | bytes accessed | tf_op | source)
XLA Modules:
  0.0 777.8 jit_solution(13866688835884828556)
XLA Ops:
  3.2 12.0 %all-to-all-start = ((f32[32,80,140]{1,2,0:T(8,128)}), f32[32,80,140]{1,2,0:T(8,128)S(1)}, u32[]{:S(2)}, u32[]{:S(2)}) async-start(f32[32,80,140]{1,2,0:T(8,128)} %stack.52), calls=%async_computation | async-start | bytes 4718592 | tf_op jit(solution)/shard_map/all_to_all | solution.py:81
  16.6 52.6 %all-to-all-done = f32[32,80,140]{1,2,0:T(8,128)S(1)} async-done(((f32[32,80,140]{1,2,0:T(8,128)}), f32[32,80,140]{1,2,0:T(8,128)S(1)}, u32[]{:S(2)}, u32[]{:S(2)}) %all-to-all-start) | async-done | bytes 1433632 | tf_op jit(solution)/shard_map/all_to_all | solution.py:81
  74.7 7.6 slice.1230
  82.4 30.2 %slice.1231 = f32[2,40,2240]{2,1,0:T(8,128)} slice(f32[2,40,4480]{2,1,0:T(8,128)} %slice.1230), slice={[0:2:1], [0:40:1], [0:4480:2]} | slice | bytes 1433600 | tf_op jit(solution)/shard_map/slice | solution.py:46
  112.5 30.2 %slice.1232 = f32[2,40,2240]{2,1,0:T(8,128)} slice(f32[2,40,4480]{2,1,0:T(8,128)} %slice.1230), slice={[0:2:1], [0:40:1], [1:4480:2]} | slice | bytes 1433600 | tf_op jit(solution)/shard_map/slice | solution.py:46
  142.7 7.6 slice.1233
  150.3 30.4 %slice.1234 = f32[2,40,2240]{2,1,0:T(8,128)} slice(f32[2,40,4480]{2,1,0:T(8,128)} %slice.1233), slice={[0:2:1], [0:40:1], [0:4480:2]} | slice | bytes 1433600 | tf_op jit(solution)/shard_map/slice | solution.py:46
  180.7 30.2 %slice.1235 = f32[2,40,2240]{2,1,0:T(8,128)} slice(f32[2,40,4480]{2,1,0:T(8,128)} %slice.1233), slice={[0:2:1], [0:40:1], [1:4480:2]} | slice | bytes 1433600 | tf_op jit(solution)/shard_map/slice | solution.py:46
  281.6 81.9 %while.64 = (s32[]{:T(128)}, f32[5,1,5,280]{3,0,2,1:T(8,128)}, f32[11]{0:T(128)S(1)}, f32[5,1,15,280]{3,2,1,0:T(8,128)S(1)}, s32[]{:T(128)}, /*index=5*/s32[]{:T(128)}) while((s32[]{:T(128)}, f32[5,1,5,280]{3,0,2,1:T(8,128)}, f32[11]{0:T(128)S(1)}, f32[5,1,15,280]{3,2,1,0:T(8,128)S(1)}, s32[]{:T(128)}, /*index=5*/s32[]{:T(128)}) %tuple.190), condition=%wide.region_10.11_spmd, body=%wide.region_9.10_spmd.sunk | while | flops 58802 | bytes 134653 | solution.py:61
  370.8 83.1 %while.63 = (s32[]{:T(128)}, f32[5,1,10,560]{3,0,2,1:T(8,128)}, f32[11]{0:T(128)S(1)}, f32[5,1,20,560]{3,2,1,0:T(8,128)S(1)}, s32[]{:T(128)}, /*index=5*/s32[]{:T(128)}) while((s32[]{:T(128)}, f32[5,1,10,560]{3,0,2,1:T(8,128)}, f32[11]{0:T(128)S(1)}, f32[5,1,20,560]{3,2,1,0:T(8,128)S(1)}, s32[]{:T(128)}, /*index=5*/s32[]{:T(128)}) %tuple.193), condition=%wide.region_8.9_spmd, body=%wide.region_7.8_spmd.sunk | while | flops 235202 | bytes 493053 | solution.py:61
  460.1 95.4 %while.62 = (s32[]{:T(128)}, f32[5,1,20,1120]{3,0,2,1:T(8,128)}, f32[11]{0:T(128)S(1)}, f32[5,1,30,1120]{3,2,1,0:T(8,128)}, s32[]{:T(128)}, /*index=5*/s32[]{:T(128)}) while((s32[]{:T(128)}, f32[5,1,20,1120]{3,0,2,1:T(8,128)}, f32[11]{0:T(128)S(1)}, f32[5,1,30,1120]{3,2,1,0:T(8,128)}, s32[]{:T(128)}, /*index=5*/s32[]{:T(128)}) %tuple.199), condition=%wide.region_6.7_spmd, body=%wide.region_5.6_spmd.sunk | while | flops 940802 | bytes 1881853 | solution.py:61
  562.2 90.0 %while.61 = (s32[]{:T(128)}, f32[5,1,40,2240]{3,2,1,0:T(8,128)}, f32[11]{0:T(128)S(1)}, f32[5,1,50,2240]{3,2,1,0:T(8,128)}, s32[]{:T(128)}) while((s32[]{:T(128)}, f32[5,1,40,2240]{3,2,1,0:T(8,128)}, f32[11]{0:T(128)S(1)}, f32[5,1,50,2240]{3,2,1,0:T(8,128)}, s32[]{:T(128)}) %tuple.198), condition=%wide.region_4.5_spmd, body=%wide.region_3.4_spmd.sunk | while | flops 3763202 | bytes 5930181 | solution.py:61
  564.0 7.4 fusion.123
  571.4 8.8 %bitcast_dynamic-update-slice_fusion.25 = f32[5,1,40,2240]{3,2,1,0:T(8,128)} fusion(f32[5,1,40,2240]{3,2,1,0:T(8,128)} %get-tuple-element.634, s32[]{:T(128)} %get-tuple-element.633, f32[1,40,2240]{2,1,0:T(8,128)S(1)} %fusion.123, f32[]{:T(128)} %bitcast.276, f32[]{:T(128)} %bitcast.277, f32[]{:T(128)} %bitcast.278, f32[]{:T(128)} %bitcast.279, ...), kind=kLoop, calls=%fused_computation.56.clone.1 | loop fusion | flops 1881600 | bytes 733184 | tf_op jit(solution)/shard_map/while/body/jit(dynamic_update_index_in_dim)/dynamic_update_slice | solution.py:61
  581.9 7.4 fusion.123
  589.4 8.8 %bitcast_dynamic-update-slice_fusion.25 = f32[5,1,40,2240]{3,2,1,0:T(8,128)} fusion(f32[5,1,40,2240]{3,2,1,0:T(8,128)} %get-tuple-element.634, s32[]{:T(128)} %get-tuple-element.633, f32[1,40,2240]{2,1,0:T(8,128)S(1)} %fusion.123, f32[]{:T(128)} %bitcast.276, f32[]{:T(128)} %bitcast.277, f32[]{:T(128)} %bitcast.278, f32[]{:T(128)} %bitcast.279, ...), kind=kLoop, calls=%fused_computation.56.clone.1 | loop fusion | flops 1881600 | bytes 733184 | tf_op jit(solution)/shard_map/while/body/jit(dynamic_update_index_in_dim)/dynamic_update_slice | solution.py:61
  599.9 7.4 fusion.123
  607.4 8.8 %bitcast_dynamic-update-slice_fusion.25 = f32[5,1,40,2240]{3,2,1,0:T(8,128)} fusion(f32[5,1,40,2240]{3,2,1,0:T(8,128)} %get-tuple-element.634, s32[]{:T(128)} %get-tuple-element.633, f32[1,40,2240]{2,1,0:T(8,128)S(1)} %fusion.123, f32[]{:T(128)} %bitcast.276, f32[]{:T(128)} %bitcast.277, f32[]{:T(128)} %bitcast.278, f32[]{:T(128)} %bitcast.279, ...), kind=kLoop, calls=%fused_computation.56.clone.1 | loop fusion | flops 1881600 | bytes 733184 | tf_op jit(solution)/shard_map/while/body/jit(dynamic_update_index_in_dim)/dynamic_update_slice | solution.py:61
  618.0 7.4 fusion.123
  625.4 8.8 %bitcast_dynamic-update-slice_fusion.25 = f32[5,1,40,2240]{3,2,1,0:T(8,128)} fusion(f32[5,1,40,2240]{3,2,1,0:T(8,128)} %get-tuple-element.634, s32[]{:T(128)} %get-tuple-element.633, f32[1,40,2240]{2,1,0:T(8,128)S(1)} %fusion.123, f32[]{:T(128)} %bitcast.276, f32[]{:T(128)} %bitcast.277, f32[]{:T(128)} %bitcast.278, f32[]{:T(128)} %bitcast.279, ...), kind=kLoop, calls=%fused_computation.56.clone.1 | loop fusion | flops 1881600 | bytes 733184 | tf_op jit(solution)/shard_map/while/body/jit(dynamic_update_index_in_dim)/dynamic_update_slice | solution.py:61
  643.4 8.8 %bitcast_dynamic-update-slice_fusion.25 = f32[5,1,40,2240]{3,2,1,0:T(8,128)} fusion(f32[5,1,40,2240]{3,2,1,0:T(8,128)} %get-tuple-element.634, s32[]{:T(128)} %get-tuple-element.633, f32[1,40,2240]{2,1,0:T(8,128)S(1)} %fusion.123, f32[]{:T(128)} %bitcast.276, f32[]{:T(128)} %bitcast.277, f32[]{:T(128)} %bitcast.278, f32[]{:T(128)} %bitcast.279, ...), kind=kLoop, calls=%fused_computation.56.clone.1 | loop fusion | flops 1881600 | bytes 733184 | tf_op jit(solution)/shard_map/while/body/jit(dynamic_update_index_in_dim)/dynamic_update_slice | solution.py:61
  659.8 112.8 %while.60 = (s32[]{:T(128)}, f32[5,1,80,4480]{3,2,1,0:T(8,128)}, f32[11]{0:T(128)S(1)}, f32[5,1,90,4480]{3,2,1,0:T(8,128)}, s32[]{:T(128)}) while((s32[]{:T(128)}, f32[5,1,80,4480]{3,2,1,0:T(8,128)}, f32[11]{0:T(128)S(1)}, f32[5,1,90,4480]{3,2,1,0:T(8,128)}, s32[]{:T(128)}) %tuple.197), condition=%wide.region_2.3_spmd, body=%wide.region_1.2_spmd.sunk | while | flops 15052802 | bytes 23302340 | solution.py:61
  662.1 8.7 %fusion.121 = f32[1,80,4480]{2,1,0:T(8,128)S(1)} fusion(f32[1,90,4480]{2,1,0:T(8,128)S(1)} %dynamic-slice_bitcast_fusion.10, f32[]{:T(128)} %bitcast.263, f32[]{:T(128)} %bitcast.264, f32[]{:T(128)} %bitcast.265, f32[]{:T(128)} %bitcast.266, f32[]{:T(128)} %bitcast.267, f32[]{:T(128)} %bitcast.268, f32[]{:T(128)} %bitcast.269, f32[]{:T(128)} %bitcast.270, ...), kind=kLoop, calls=%fused_computation.2.clone.1 | loop fusion | flops 7526400 | bytes 17203244 | tf_op jit(solution)/shard_map/while/body/eval_jaxpr/add | solution.py:34
  670.8 11.6 %bitcast_dynamic-update-slice_fusion.24 = f32[5,1,80,4480]{3,2,1,0:T(8,128)} fusion(f32[5,1,80,4480]{3,2,1,0:T(8,128)} %get-tuple-element.619, s32[]{:T(128)} %get-tuple-element.618, f32[1,80,4480]{2,1,0:T(8,128)S(1)} %fusion.121, f32[]{:T(128)} %bitcast.263, f32[]{:T(128)} %bitcast.264, f32[]{:T(128)} %bitcast.265, f32[]{:T(128)} %bitcast.266, ...), kind=kLoop, calls=%fused_computation.22.clone.1 | loop fusion | flops 7526400 | bytes 2873344 | tf_op jit(solution)/shard_map/while/body/jit(dynamic_update_index_in_dim)/dynamic_update_slice | solution.py:61
  684.7 8.7 %fusion.121 = f32[1,80,4480]{2,1,0:T(8,128)S(1)} fusion(f32[1,90,4480]{2,1,0:T(8,128)S(1)} %dynamic-slice_bitcast_fusion.10, f32[]{:T(128)} %bitcast.263, f32[]{:T(128)} %bitcast.264, f32[]{:T(128)} %bitcast.265, f32[]{:T(128)} %bitcast.266, f32[]{:T(128)} %bitcast.267, f32[]{:T(128)} %bitcast.268, f32[]{:T(128)} %bitcast.269, f32[]{:T(128)} %bitcast.270, ...), kind=kLoop, calls=%fused_computation.2.clone.1 | loop fusion | flops 7526400 | bytes 17203244 | tf_op jit(solution)/shard_map/while/body/eval_jaxpr/add | solution.py:34
  693.4 11.5 %bitcast_dynamic-update-slice_fusion.24 = f32[5,1,80,4480]{3,2,1,0:T(8,128)} fusion(f32[5,1,80,4480]{3,2,1,0:T(8,128)} %get-tuple-element.619, s32[]{:T(128)} %get-tuple-element.618, f32[1,80,4480]{2,1,0:T(8,128)S(1)} %fusion.121, f32[]{:T(128)} %bitcast.263, f32[]{:T(128)} %bitcast.264, f32[]{:T(128)} %bitcast.265, f32[]{:T(128)} %bitcast.266, ...), kind=kLoop, calls=%fused_computation.22.clone.1 | loop fusion | flops 7526400 | bytes 2873344 | tf_op jit(solution)/shard_map/while/body/jit(dynamic_update_index_in_dim)/dynamic_update_slice | solution.py:61
  707.2 8.7 %fusion.121 = f32[1,80,4480]{2,1,0:T(8,128)S(1)} fusion(f32[1,90,4480]{2,1,0:T(8,128)S(1)} %dynamic-slice_bitcast_fusion.10, f32[]{:T(128)} %bitcast.263, f32[]{:T(128)} %bitcast.264, f32[]{:T(128)} %bitcast.265, f32[]{:T(128)} %bitcast.266, f32[]{:T(128)} %bitcast.267, f32[]{:T(128)} %bitcast.268, f32[]{:T(128)} %bitcast.269, f32[]{:T(128)} %bitcast.270, ...), kind=kLoop, calls=%fused_computation.2.clone.1 | loop fusion | flops 7526400 | bytes 17203244 | tf_op jit(solution)/shard_map/while/body/eval_jaxpr/add | solution.py:34
  716.0 11.5 %bitcast_dynamic-update-slice_fusion.24 = f32[5,1,80,4480]{3,2,1,0:T(8,128)} fusion(f32[5,1,80,4480]{3,2,1,0:T(8,128)} %get-tuple-element.619, s32[]{:T(128)} %get-tuple-element.618, f32[1,80,4480]{2,1,0:T(8,128)S(1)} %fusion.121, f32[]{:T(128)} %bitcast.263, f32[]{:T(128)} %bitcast.264, f32[]{:T(128)} %bitcast.265, f32[]{:T(128)} %bitcast.266, ...), kind=kLoop, calls=%fused_computation.22.clone.1 | loop fusion | flops 7526400 | bytes 2873344 | tf_op jit(solution)/shard_map/while/body/jit(dynamic_update_index_in_dim)/dynamic_update_slice | solution.py:61
  729.8 8.7 %fusion.121 = f32[1,80,4480]{2,1,0:T(8,128)S(1)} fusion(f32[1,90,4480]{2,1,0:T(8,128)S(1)} %dynamic-slice_bitcast_fusion.10, f32[]{:T(128)} %bitcast.263, f32[]{:T(128)} %bitcast.264, f32[]{:T(128)} %bitcast.265, f32[]{:T(128)} %bitcast.266, f32[]{:T(128)} %bitcast.267, f32[]{:T(128)} %bitcast.268, f32[]{:T(128)} %bitcast.269, f32[]{:T(128)} %bitcast.270, ...), kind=kLoop, calls=%fused_computation.2.clone.1 | loop fusion | flops 7526400 | bytes 17203244 | tf_op jit(solution)/shard_map/while/body/eval_jaxpr/add | solution.py:34
  738.5 11.6 %bitcast_dynamic-update-slice_fusion.24 = f32[5,1,80,4480]{3,2,1,0:T(8,128)} fusion(f32[5,1,80,4480]{3,2,1,0:T(8,128)} %get-tuple-element.619, s32[]{:T(128)} %get-tuple-element.618, f32[1,80,4480]{2,1,0:T(8,128)S(1)} %fusion.121, f32[]{:T(128)} %bitcast.263, f32[]{:T(128)} %bitcast.264, f32[]{:T(128)} %bitcast.265, f32[]{:T(128)} %bitcast.266, ...), kind=kLoop, calls=%fused_computation.22.clone.1 | loop fusion | flops 7526400 | bytes 2873344 | tf_op jit(solution)/shard_map/while/body/jit(dynamic_update_index_in_dim)/dynamic_update_slice | solution.py:61
  752.3 8.7 %fusion.121 = f32[1,80,4480]{2,1,0:T(8,128)S(1)} fusion(f32[1,90,4480]{2,1,0:T(8,128)S(1)} %dynamic-slice_bitcast_fusion.10, f32[]{:T(128)} %bitcast.263, f32[]{:T(128)} %bitcast.264, f32[]{:T(128)} %bitcast.265, f32[]{:T(128)} %bitcast.266, f32[]{:T(128)} %bitcast.267, f32[]{:T(128)} %bitcast.268, f32[]{:T(128)} %bitcast.269, f32[]{:T(128)} %bitcast.270, ...), kind=kLoop, calls=%fused_computation.2.clone.1 | loop fusion | flops 7526400 | bytes 17203244 | tf_op jit(solution)/shard_map/while/body/eval_jaxpr/add | solution.py:34
  761.1 11.5 %bitcast_dynamic-update-slice_fusion.24 = f32[5,1,80,4480]{3,2,1,0:T(8,128)} fusion(f32[5,1,80,4480]{3,2,1,0:T(8,128)} %get-tuple-element.619, s32[]{:T(128)} %get-tuple-element.618, f32[1,80,4480]{2,1,0:T(8,128)S(1)} %fusion.121, f32[]{:T(128)} %bitcast.263, f32[]{:T(128)} %bitcast.264, f32[]{:T(128)} %bitcast.265, f32[]{:T(128)} %bitcast.266, ...), kind=kLoop, calls=%fused_computation.22.clone.1 | loop fusion | flops 7526400 | bytes 2873344 | tf_op jit(solution)/shard_map/while/body/jit(dynamic_update_index_in_dim)/dynamic_update_slice | solution.py:61
  (211 shorter events, 399.7 us)
Async XLA Ops:
  3.2 65.9 %all-to-all-start = ((f32[32,80,140]{1,2,0:T(8,128)}), f32[32,80,140]{1,2,0:T(8,128)S(1)}, u32[]{:S(2)}, u32[]{:S(2)}) async-start(f32[32,80,140]{1,2,0:T(8,128)} %stack.52), calls=%async_computation | async-start | bytes 4718592 | tf_op jit(solution)/shard_map/all_to_all | solution.py:81
  70.7 2.3 copy-start
  255.7 20.1 %collective-permute-start.8 = (f32[2,5,280]{2,1,0:T(8,128)S(1)}, f32[2,5,280]{2,1,0:T(8,128)S(1)}, u32[]{:S(2)}, u32[]{:S(2)}) collective-permute-start(f32[2,5,280]{2,1,0:T(8,128)S(1)} %add_multiply_fusion.3), channel_id=1, source_target_pairs={{0,1},{1,2},{2,3},{3,4},{4,5},{5,6},{6,7},{8,9},{9,10},{10,11},{11... | collective-permute-start | bytes 33608 | tf_op jit(solution)/shard_map/ppermute | solution.py:15
  261.5 16.3 %collective-permute-start.9 = (f32[2,5,280]{2,1,0:T(8,128)S(1)}, f32[2,5,280]{2,1,0:T(8,128)S(1)}, u32[]{:S(2)}, u32[]{:S(2)}) collective-permute-start(f32[2,5,280]{2,1,0:T(8,128)S(1)} %add_multiply_fusion.3), channel_id=1, source_target_pairs={{1,0},{2,1},{3,2},{4,3},{5,4},{6,5},{7,6},{9,8},{10,9},{11,10},{12... | collective-permute-start | bytes 33608 | tf_op jit(solution)/shard_map/ppermute | solution.py:18
  266.6 98.5 %collective-permute-start.6 = (f32[2,5,560]{2,1,0:T(8,128)S(1)}, f32[2,5,560]{2,1,0:T(8,128)S(1)}, u32[]{:S(2)}, u32[]{:S(2)}) collective-permute-start(f32[2,5,560]{2,1,0:T(8,128)S(1)} %get-tuple-element.376), channel_id=1, source_target_pairs={{0,1},{1,2},{2,3},{3,4},{4,5},{5,6},{6,7},{8,9},{9,10},{10,11},{11... | collective-permute-start | bytes 67208 | tf_op jit(solution)/shard_map/ppermute | solution.py:15
  270.3 96.8 %collective-permute-start.7 = (f32[2,5,560]{2,1,0:T(8,128)S(1)}, f32[2,5,560]{2,1,0:T(8,128)S(1)}, u32[]{:S(2)}, u32[]{:S(2)}) collective-permute-start(f32[2,5,560]{2,1,0:T(8,128)S(1)} %get-tuple-element.377), channel_id=1, source_target_pairs={{1,0},{2,1},{3,2},{4,3},{5,4},{6,5},{7,6},{9,8},{10,9},{11,10},{12... | collective-permute-start | bytes 67208 | tf_op jit(solution)/shard_map/ppermute | solution.py:18
  272.2 184.0 %collective-permute-start.4 = (f32[2,5,1120]{2,1,0:T(8,128)}, f32[2,5,1120]{2,1,0:T(8,128)}, u32[]{:S(2)}, u32[]{:S(2)}) collective-permute-start(f32[2,5,1120]{2,1,0:T(8,128)} %get-tuple-element.374), channel_id=1, source_target_pairs={{0,1},{1,2},{2,3},{3,4},{4,5},{5,6},{6,7},{8,9},{9,10},{10,11},{11... | collective-permute-start | bytes 134408 | tf_op jit(solution)/shard_map/ppermute | solution.py:15
  275.9 182.2 %collective-permute-start.5 = (f32[2,5,1120]{2,1,0:T(8,128)S(1)}, f32[2,5,1120]{2,1,0:T(8,128)}, u32[]{:S(2)}, u32[]{:S(2)}) collective-permute-start(f32[2,5,1120]{2,1,0:T(8,128)S(1)} %get-tuple-element.375), channel_id=1, source_target_pairs={{1,0},{2,1},{3,2},{4,3},{5,4},{6,5},{7,6},{9,8},{10,9},{11,10},{12... | collective-permute-start | bytes 134408 | tf_op jit(solution)/shard_map/ppermute | solution.py:18
  277.8 281.2 %collective-permute-start.2 = (f32[2,5,2240]{2,1,0:T(8,128)}, f32[2,5,2240]{2,1,0:T(8,128)}, u32[]{:S(2)}, u32[]{:S(2)}) collective-permute-start(f32[2,5,2240]{2,1,0:T(8,128)} %get-tuple-element.372), channel_id=1, source_target_pairs={{0,1},{1,2},{2,3},{3,4},{4,5},{5,6},{6,7},{8,9},{9,10},{10,11},{11... | collective-permute-start | bytes 268808 | tf_op jit(solution)/shard_map/ppermute | solution.py:15
  365.1 193.9 %collective-permute-start.3 = (f32[2,5,2240]{2,1,0:T(8,128)}, f32[2,5,2240]{2,1,0:T(8,128)}, u32[]{:S(2)}, u32[]{:S(2)}) collective-permute-start(f32[2,5,2240]{2,1,0:T(8,128)} %get-tuple-element.373), channel_id=1, source_target_pairs={{1,0},{2,1},{3,2},{4,3},{5,4},{6,5},{7,6},{9,8},{10,9},{11,10},{12... | collective-permute-start | bytes 268808 | tf_op jit(solution)/shard_map/ppermute | solution.py:18
  367.1 287.5 %collective-permute-start = (f32[2,5,4480]{2,1,0:T(8,128)}, f32[2,5,4480]{2,1,0:T(8,128)}, u32[]{:S(2)}, u32[]{:S(2)}) collective-permute-start(f32[2,5,4480]{2,1,0:T(8,128)} %get-tuple-element.370), channel_id=1, source_target_pairs={{0,1},{1,2},{2,3},{3,4},{4,5},{5,6},{6,7},{8,9},{9,10},{10,11},{11... | collective-permute-start | bytes 537608 | tf_op jit(solution)/shard_map/ppermute | solution.py:15
  456.2 198.3 %collective-permute-start.1 = (f32[2,5,4480]{2,1,0:T(8,128)}, f32[2,5,4480]{2,1,0:T(8,128)S(1)}, u32[]{:S(2)}, u32[]{:S(2)}) collective-permute-start(f32[2,5,4480]{2,1,0:T(8,128)} %get-tuple-element.371), channel_id=1, source_target_pairs={{1,0},{2,1},{3,2},{4,3},{5,4},{6,5},{7,6},{9,8},{10,9},{11,10},{12... | collective-permute-start | bytes 537608 | tf_op jit(solution)/shard_map/ppermute | solution.py:18
  459.2 0.9 copy-start.3
  560.6 1.6 copy-start.2
  656.5 3.3 copy-start.1
